TPU v7x, 32 devices: a whole 2x2x4 slice. The times are simulated.
32 devices in a mesh: dp: 8 (over z, y), tensor: 4 (over x, core).
Axes of the slice: x: 2, y: 2, z: 4, core: 2. Of those that a mesh axis runs over, the one named last changes fastest.
Arguments:
- layer_input: bfloat16 [10240, 768], P(('dp', 'tensor')), may hold values from -6 to 6
- cotangent: bfloat16 [10240, 768], P(('dp', 'tensor')), may hold values from -6 to 6
- segments: int32 [10240], replicated, may hold values from 0 to 25, as said below
- parents: int32 [26], replicated, may hold values from 0 to 17, as said below
- norm1_gain: bfloat16 [768], P('dp'), may hold values from 0.099609375 to 1.8984375
- w_query: bfloat16 [768, 768], P('dp', 'tensor'), may hold values from -0.21875 to 0.21875
- w_key: bfloat16 [768, 768], P('dp', 'tensor'), may hold values from -0.21875 to 0.21875
- w_value: bfloat16 [768, 768], P('dp', 'tensor'), may hold values from -0.21875 to 0.21875
- w_out: bfloat16 [768, 768], P('tensor', 'dp'), may hold values from -1.75 to 1.75
- norm2_gain: bfloat16 [768], P('dp'), may hold values from 0.099609375 to 1.8984375
- w_up: bfloat16 [768, 3072], P('dp', 'tensor'), may hold values from -0.21875 to 0.21875
- w_down: bfloat16 [3072, 768], P('tensor', 'dp'), may hold values from -0.109375 to 0.109375
Outputs:
- layer_output: bfloat16 [10240, 768], P(('dp', 'tensor'))
- input_grad: bfloat16 [10240, 768], P(('dp', 'tensor'))
- grad_norm1_gain: float32 [768], P('dp')
- grad_query: float32 [768, 768], P('dp', 'tensor')
- grad_key: float32 [768, 768], P('dp', 'tensor')
- grad_value: float32 [768, 768], P('dp', 'tensor')
- grad_out: float32 [768, 768], P('tensor', 'dp')
- grad_norm2_gain: float32 [768], P('dp')
- grad_up: float32 [768, 3072], P('dp', 'tensor')
- grad_down: float32 [3072, 768], P('tensor', 'dp')
Inputs may be any that keep to these rules, and one draw needn't show every extreme that they name: Tree t holds bytes 5120 t to 5120 (t + 1) - 1 of the stream (the last tree may end at 10240). Its first 2048 bytes are segment 13 t, the trunk; the rest are twelve runs of 256 bytes with the segments 13 t + 1 to 13 t + 12 in some order, every run after the run of its parent segment. parents[s] is the parent segment of s: the trunk 13 t is its own parent, the branches 13 t + 1 to 13 t + 4 have the trunk, and the leaves 13 t + 5 to 13 t + 12 have one of the four branches each, two leaves a branch.
All inputs are finite; a program needn't handle non-finite values.
Results may differ from a plain program's by a relative error of at most 0.017.
Values may be sent and summed in bfloat16 or wider, within the bound.
A program may use at most 256 MiB of HBM per device.

v0:
```python
import math
import jax
import jax.numpy as jnp
from jax import lax
from jax.sharding import PartitionSpec as P

HD = 64
WINDOW = 1536
epsilon = 1e-06
masked_score = -1e30


def from_behind(block, axis, distance):
    devices = range(lax.axis_size(axis))
    route = [(i - distance, i) for i in devices if i - distance in devices]
    return lax.ppermute(block, axis, route)


def split_up(x, dim, peers):
    dims = x.shape
    tiles = x.reshape(*dims[:dim], peers, dims[dim] // peers, *dims[dim + 1 :])
    return jnp.moveaxis(tiles, dim, 0)


def sum_at_owner(x, axis, dim):
    tiles = split_up(x, dim, lax.axis_size(axis))
    arrived = lax.all_to_all(tiles, axis, split_axis=0, concat_axis=0, tiled=True)
    return arrived.astype(jnp.float32).sum(axis=0)


def side_by_side(arrays, axis, dim, along):
    widths = [math.prod(a.shape[along:]) for a in arrays]
    both = jnp.concatenate(
        [a.reshape(*a.shape[:along], w) for a, w in zip(arrays, widths)], axis=along
    )
    whole = sum_at_owner(both, axis, dim)
    tiles = jnp.split(whole, [sum(widths[:k]) for k in range(1, len(widths))], axis=along)
    return tuple((b.reshape(*whole.shape[:along], *a.shape[along:]) for a, b in zip(arrays, tiles)))


def gelu_exact(values):
    return jax.nn.gelu(values, approximate=False)


def row_scale(values):
    return lax.rsqrt(jnp.mean(values * values, axis=-1, keepdims=True) + epsilon)


def norm_backward(incoming, normal_hat, row_factor, gain):
    scaled = incoming * gain
    inner = jnp.mean(scaled * normal_hat, axis=-1, keepdims=True)
    return (row_factor * (scaled - normal_hat * inner), jnp.sum(incoming * normal_hat, axis=0))


def parent_of(seg_ids, parents):
    seg_table = jnp.arange(parents.shape[0], dtype=jnp.int32)
    hits = seg_ids[:, None] == seg_table[None, :]
    return jnp.sum(jnp.where(hits, parents[None, :], 0), axis=1)


def shards(
    layer_input,
    cotangent,
    segments,
    parents,
    norm1_gain,
    w_query,
    w_key,
    w_value,
    w_out,
    norm2_gain,
    w_up,
    w_down,
):
    gain_one, full_query, full_key, full_value, full_out, gain_two, full_up, full_down = (
        lax.all_gather(norm1_gain, "dp", axis=0, tiled=True),
        lax.all_gather(w_query, "dp", axis=0, tiled=True),
        lax.all_gather(w_key, "dp", axis=0, tiled=True),
        lax.all_gather(w_value, "dp", axis=0, tiled=True),
        lax.all_gather(w_out, "dp", axis=1, tiled=True),
        lax.all_gather(norm2_gain, "dp", axis=0, tiled=True),
        lax.all_gather(w_up, "dp", axis=0, tiled=True),
        lax.all_gather(w_down, "dp", axis=1, tiled=True),
    )
    gain_one = gain_one.astype(jnp.float32)
    gain_two = gain_two.astype(jnp.float32)
    row_count = layer_input.shape[0]
    token_count = row_count * lax.axis_size("tensor")
    position = lax.axis_index("dp") * token_count
    head_width = full_query.shape[1]
    head_count = head_width // HD
    scaling = HD ** (-0.5)
    block_rows = min(640, token_count)
    block_count = token_count // block_rows
    span = WINDOW + block_rows
    hop_count = (WINDOW + token_count - 1) // token_count
    inputs = layer_input.astype(jnp.float32)
    factor_one = row_scale(inputs)
    hat_one = inputs * factor_one
    normed = (hat_one * gain_one).astype(jnp.bfloat16)
    normed_all = lax.all_gather(normed, "tensor", axis=0, tiled=True)
    queries = jnp.dot(normed_all, full_query, preferred_element_type=jnp.float32).astype(
        jnp.bfloat16
    )
    keys_own = jnp.dot(normed_all, full_key, preferred_element_type=jnp.float32).astype(
        jnp.bfloat16
    )
    values_own = jnp.dot(normed_all, full_value, preferred_element_type=jnp.float32).astype(
        jnp.bfloat16
    )
    pair_own = jnp.concatenate([keys_own, values_own], axis=1)
    halo_parts = []
    for distance in range(1, hop_count + 1):
        length = min(token_count, WINDOW - (distance - 1) * token_count)
        piece = pair_own[token_count - length :]
        moved = from_behind(piece, "dp", distance)
        halo_parts.append(moved)
    pair_all = jnp.concatenate(halo_parts[::-1] + [pair_own], axis=0)
    seg_padded = jnp.concatenate([jnp.full((WINDOW,), -1, jnp.int32), segments])
    seg_keys = lax.dynamic_slice_in_dim(seg_padded, position, WINDOW + token_count, 0)
    seg_query = seg_keys[WINDOW:]
    parent_one = parent_of(seg_query, parents)
    parent_two = parent_of(parent_one, parents)
    query_spots = jnp.arange(block_rows, dtype=jnp.int32)
    key_spots = jnp.arange(span, dtype=jnp.int32)

    def scores_of(offset):
        query_block = lax.dynamic_slice_in_dim(queries, offset, block_rows, 0).reshape(
            block_rows, head_count, HD
        )
        pair_block = lax.dynamic_slice_in_dim(pair_all, offset, span, 0)
        key_block = pair_block[:, :head_width].reshape(span, head_count, HD)
        value_block = pair_block[:, head_width:].reshape(span, head_count, HD)
        own_seg = lax.dynamic_slice_in_dim(seg_query, offset, block_rows, 0)
        up_one = lax.dynamic_slice_in_dim(parent_one, offset, block_rows, 0)
        up_two = lax.dynamic_slice_in_dim(parent_two, offset, block_rows, 0)
        near_seg = lax.dynamic_slice_in_dim(seg_keys, offset, span, 0)
        gap = WINDOW + query_spots[:, None] - key_spots[None, :]
        same_path = (
            (near_seg[None, :] == own_seg[:, None])
            | (near_seg[None, :] == up_one[:, None])
            | (near_seg[None, :] == up_two[:, None])
        )
        allowed = (gap >= 0) & (gap < WINDOW) & same_path
        raw = (
            jnp.einsum("qhd,khd->hqk", query_block, key_block, preferred_element_type=jnp.float32)
            * scaling
        )
        return (jnp.where(allowed[None], raw, masked_score), query_block, key_block, value_block)

    def forward_block(block_index):
        scores, query_block, key_block, value_block = scores_of(block_index * block_rows)
        row_max = jnp.max(scores, axis=-1, keepdims=True)
        exponent = jnp.exp(scores - row_max)
        denominator = jnp.sum(exponent, axis=-1, keepdims=True)
        weights = (exponent / denominator).astype(jnp.bfloat16)
        mixed = jnp.einsum("hqk,khd->qhd", weights, value_block, preferred_element_type=jnp.float32)
        return (
            mixed.reshape(block_rows, head_width).astype(jnp.bfloat16),
            (row_max + jnp.log(denominator))[..., 0],
        )

    context_blocks, logsum_blocks = lax.map(forward_block, jnp.arange(block_count, dtype=jnp.int32))
    context = context_blocks.reshape(token_count, head_width)
    middle = inputs + lax.psum_scatter(
        jnp.dot(context, full_out, preferred_element_type=jnp.float32).astype(jnp.bfloat16),
        "tensor",
        scatter_dimension=0,
        tiled=True,
    ).astype(jnp.float32)
    factor_two = row_scale(middle)
    hat_two = middle * factor_two
    normed_two = (hat_two * gain_two).astype(jnp.bfloat16)
    normed_two_all = lax.all_gather(normed_two, "tensor", axis=0, tiled=True)
    upper = jnp.dot(normed_two_all, full_up, preferred_element_type=jnp.float32)
    active = gelu_exact(upper).astype(jnp.bfloat16)
    result = middle + lax.psum_scatter(
        jnp.dot(active, full_down, preferred_element_type=jnp.float32).astype(jnp.bfloat16),
        "tensor",
        scatter_dimension=0,
        tiled=True,
    ).astype(jnp.float32)
    incoming = cotangent.astype(jnp.float32)
    incoming_all = lax.all_gather(cotangent, "tensor", axis=0, tiled=True)
    grad_down = jnp.einsum("tf,td->fd", active, incoming_all, preferred_element_type=jnp.float32)
    grad_active = jnp.einsum(
        "td,fd->tf", incoming_all, full_down, preferred_element_type=jnp.float32
    )
    unused_value, gelu_pull = jax.vjp(gelu_exact, upper)
    grad_upper = gelu_pull(grad_active)[0].astype(jnp.bfloat16)
    grad_up = jnp.einsum(
        "tc,tf->cf", normed_two_all, grad_upper, preferred_element_type=jnp.float32
    )
    grad_normed_two = lax.psum_scatter(
        jnp.einsum("tf,cf->tc", grad_upper, full_up, preferred_element_type=jnp.float32).astype(
            jnp.bfloat16
        ),
        "tensor",
        scatter_dimension=0,
        tiled=True,
    ).astype(jnp.float32)
    through_two, gain_two_part = norm_backward(grad_normed_two, hat_two, factor_two, gain_two)
    grad_middle = incoming + through_two
    grad_middle_all = lax.all_gather(grad_middle.astype(jnp.bfloat16), "tensor", axis=0, tiled=True)
    grad_out = jnp.einsum("tc,td->cd", context, grad_middle_all, preferred_element_type=jnp.float32)
    grad_context = jnp.einsum(
        "td,cd->tc", grad_middle_all, full_out, preferred_element_type=jnp.float32
    ).astype(jnp.bfloat16)

    def backward_block(block_index, carry):
        grad_queries, grad_pairs = carry
        offset = block_index * block_rows
        scores, query_block, key_block, value_block = scores_of(offset)
        logsum = lax.dynamic_index_in_dim(logsum_blocks, block_index, 0, keepdims=False)
        probs = jnp.exp(scores - logsum[..., None])
        grad_rows = lax.dynamic_slice_in_dim(grad_context, offset, block_rows, 0).reshape(
            block_rows, head_count, HD
        )
        grad_probs = jnp.einsum(
            "qhd,khd->hqk", grad_rows, value_block, preferred_element_type=jnp.float32
        )
        inner = jnp.sum(probs * grad_probs, axis=-1, keepdims=True)
        grad_scores = (probs * (grad_probs - inner)).astype(jnp.bfloat16)
        grad_query_block = (
            jnp.einsum("hqk,khd->qhd", grad_scores, key_block, preferred_element_type=jnp.float32)
            * scaling
        )
        grad_key_block = (
            jnp.einsum("hqk,qhd->khd", grad_scores, query_block, preferred_element_type=jnp.float32)
            * scaling
        )
        grad_value_block = jnp.einsum(
            "hqk,qhd->khd",
            probs.astype(jnp.bfloat16),
            grad_rows,
            preferred_element_type=jnp.float32,
        )
        grad_queries = lax.dynamic_update_slice_in_dim(
            grad_queries, grad_query_block.reshape(block_rows, head_width), offset, 0
        )
        update = jnp.concatenate(
            [grad_key_block.reshape(span, head_width), grad_value_block.reshape(span, head_width)],
            axis=1,
        )
        current = lax.dynamic_slice_in_dim(grad_pairs, offset, span, 0)
        grad_pairs = lax.dynamic_update_slice_in_dim(grad_pairs, current + update, offset, 0)
        return (grad_queries, grad_pairs)

    start_carry = (
        jnp.zeros((token_count, head_width), jnp.float32),
        jnp.zeros((WINDOW + token_count, 2 * head_width), jnp.float32),
    )
    grad_queries, grad_pairs = lax.fori_loop(0, block_count, backward_block, start_carry)
    grad_own = grad_pairs[WINDOW:]
    for distance in range(1, hop_count + 1):
        length = min(token_count, WINDOW - (distance - 1) * token_count)
        first_row = WINDOW - (distance - 1) * token_count - length
        piece = grad_pairs[first_row : first_row + length]
        returned = from_behind(piece.astype(jnp.bfloat16), "dp", -distance).astype(piece.dtype)
        grad_own = grad_own + jnp.pad(returned, ((token_count - length, 0), (0, 0)))
    grad_keys = grad_own[:, :head_width].astype(jnp.bfloat16)
    grad_values = grad_own[:, head_width:].astype(jnp.bfloat16)
    grad_queries_low = grad_queries.astype(jnp.bfloat16)
    grad_query = jnp.einsum(
        "tc,tq->cq", normed_all, grad_queries_low, preferred_element_type=jnp.float32
    )
    grad_key = jnp.einsum("tc,tq->cq", normed_all, grad_keys, preferred_element_type=jnp.float32)
    grad_value = jnp.einsum(
        "tc,tq->cq", normed_all, grad_values, preferred_element_type=jnp.float32
    )
    part_query = jnp.einsum(
        "tq,cq->tc", grad_queries_low, full_query, preferred_element_type=jnp.float32
    )
    part_key = jnp.einsum("tq,cq->tc", grad_keys, full_key, preferred_element_type=jnp.float32)
    part_value = jnp.einsum(
        "tq,cq->tc", grad_values, full_value, preferred_element_type=jnp.float32
    )
    grad_normed = lax.psum_scatter(
        (part_query + part_key + part_value).astype(jnp.bfloat16),
        "tensor",
        scatter_dimension=0,
        tiled=True,
    ).astype(jnp.float32)
    through_one, gain_one_part = norm_backward(grad_normed, hat_one, factor_one, gain_one)
    grad_inputs = grad_middle + through_one
    gain_one_sum, gain_two_sum = lax.psum((gain_one_part, gain_two_part), "tensor")
    summed = (
        *side_by_side(
            (
                gain_one_sum.astype(jnp.bfloat16),
                grad_query.astype(jnp.bfloat16),
                grad_key.astype(jnp.bfloat16),
                grad_value.astype(jnp.bfloat16),
            ),
            "dp",
            0,
            1,
        ),
        sum_at_owner(grad_out.astype(jnp.bfloat16), "dp", 1),
        *side_by_side(
            (gain_two_sum.astype(jnp.bfloat16), grad_up.astype(jnp.bfloat16)), "dp", 0, 1
        ),
        sum_at_owner(grad_down.astype(jnp.bfloat16), "dp", 1),
    )
    return (
        result.astype(jnp.bfloat16),
        grad_inputs.astype(jnp.bfloat16),
        summed[0],
        summed[1],
        summed[2],
        summed[3],
        summed[4],
        summed[5],
        summed[6],
        summed[7],
    )


def solution(mesh):
    return jax.shard_map(
        shards,
        mesh=mesh,
        in_specs=(
            P(("dp", "tensor"), None),
            P(("dp", "tensor"), None),
            P(),
            P(),
            P("dp"),
            P("dp", "tensor"),
            P("dp", "tensor"),
            P("dp", "tensor"),
            P("tensor", "dp"),
            P("dp"),
            P("dp", "tensor"),
            P("tensor", "dp"),
        ),
        out_specs=(
            P(("dp", "tensor"), None),
            P(("dp", "tensor"), None),
            P("dp"),
            P("dp", "tensor"),
            P("dp", "tensor"),
            P("dp", "tensor"),
            P("tensor", "dp"),
            P("dp"),
            P("dp", "tensor"),
            P("tensor", "dp"),
        ),
        check_vma=False,
    )
```

profile of v0, /device:TPU:0, one launch (start us, length us, event | category | flops | bytes accessed | tf_op | source)
XLA Modules:
  0.0 772.6 jit_solution(16327131825716059331)
XLA Ops:
  12.9 23.7 %all-reduce.5 = (bf16[768]{0:T(1024)(128)(2,1)S(1)}, bf16[768]{0:T(1024)(128)(2,1)}) all-reduce(bf16[768]{0:T(1024)(128)(2,1)S(1)} %dynamic-update-slice, bf16[768]{0:T(1024)(128)(2,1)S(1)} %dynamic-update-slice.1), channel_id=1, replica_groups=mesh['dp'=8,'tensor'=4] {'dp'}, use_global_device_ids=true, to_apply=%add.2 | all-reduce | flops 1536 | bytes 6144
  41.0 31.2 %all_gather.38 = bf16[768,192]{1,0:T(8,128)(2,1)S(1)} all-gather(bf16[96,192]{1,0:T(8,128)(2,1)} %param.22), channel_id=1, replica_groups=mesh['dp'=8,'tensor'=4] {'dp'}, dimensions={0}, use_global_device_ids=true | all-gather | bytes 331776 | tf_op jit(solution)/shard_map/all_gather | solution.py:78
  72.2 31.2 %all_gather.39 = bf16[768,192]{1,0:T(8,128)(2,1)S(1)} all-gather(bf16[96,192]{1,0:T(8,128)(2,1)} %param.23), channel_id=1, replica_groups=mesh['dp'=8,'tensor'=4] {'dp'}, dimensions={0}, use_global_device_ids=true | all-gather | bytes 331776 | tf_op jit(solution)/shard_map/all_gather | solution.py:79
  110.2 46.0 %all_gather.41 = bf16[192,768]{0,1:T(8,128)(2,1)} all-gather(bf16[192,96]{0,1:T(8,128)(2,1)S(1)} %copy.48), channel_id=1, replica_groups=mesh['dp'=8,'tensor'=4] {'dp'}, dimensions={1}, use_global_device_ids=true | all-gather | bytes 331776 | tf_op jit(solution)/shard_map/all_gather | solution.py:80
  156.2 31.0 %all_gather.40 = bf16[768,192]{1,0:T(8,128)(2,1)S(1)} all-gather(bf16[96,192]{1,0:T(8,128)(2,1)S(1)} %copy-done.35), channel_id=1, replica_groups=mesh['dp'=8,'tensor'=4] {'dp'}, dimensions={0}, use_global_device_ids=true | all-gather | bytes 331776 | tf_op jit(solution)/shard_map/all_gather | solution.py:77
  193.2 72.5 %while.29 = (s32[]{:T(128)}, bf16[2,640,192]{1,2,0:T(8,128)(2,1)}, f32[2,3,640]{2,1,0:T(4,128)S(1)}, s32[2]{0:T(128)S(1)}, bf16[2816,384]{0,1:T(8,128)(2,1)}, /*...) while((s32[]{:T(128)}, bf16[2,640,192]{1,2,0:T(8,128)(2,1)}, ...), condition=%wide.region_6.7_spmd.clone, body=%wide.region_3.6_spmd.clone.sunk | while | flops 1133730560 | bytes 66249560 | solution.py:163
  195.0 4.8 fusion.135
  201.3 8.0 %fusion.136 = (f32[3,640]{1,0:T(4,128)S(1)}, f32[3,640,2176]{2,1,0:T(8,128)}) fusion(pred[640,2176]{1,0:T(8,128)(4,1)S(1)} %fusion.135, bf16[640,3,64]{0,2,1:T(8,128)(2,1)S(1)} %bitcast.146, bf16[2176,3,64]{0,2,1:T(8,128)(2,1)S(1)} %bitcast.145), kind=kOutput, calls=%fused_computation.7.clone.1 | convolution fusion | flops 547305600 | bytes 19193344 | tf_op jit(solution)/shard_map/while/body/eval_jaxpr/qhd,khd->hqk/dot_general | solution.py:146
  209.3 10.5 %fusion.137 = f32[3,640]{1,0:T(4,128)S(1)} fusion(f32[3,640,2176]{2,1,0:T(8,128)} %get-tuple-element.566, f32[3,640]{1,0:T(4,128)S(1)} %get-tuple-element.567, pred[640,2176]{1,0:T(8,128)(4,1)S(1)} %fusion.135), kind=kLoop, calls=%fused_computation.8.clone.1 | loop fusion | flops 16709760 | bytes 18119680 | tf_op jit(solution)/shard_map/while/body/eval_jaxpr/reduce_sum | solution.py:155
  219.8 8.8 %fusion.138 = bf16[3,64,640]{2,1,0:T(8,128)(2,1)S(1)} fusion(bf16[2176,3,64]{0,2,1:T(8,128)(2,1)S(1)} %bitcast.144, f32[3,640,2176]{2,1,0:T(8,128)} %get-tuple-element.566, f32[3,640]{1,0:T(4,128)S(1)} %fusion.137, f32[3,640]{1,0:T(4,128)S(1)} %get-tuple-element.567, pred[640,2176]{1,0:T(8,128)(4,1)S(1)} %fusion.135), kind=kOutput, calls=%fused_computation.15.clone.1 | convolution fusion | flops 555786240 | bytes 19201024 | tf_op jit(solution)/shard_map/while/body/eval_jaxpr/hqk,khd->qhd/dot_general | solution.py:157
  231.1 4.8 fusion.135
  237.5 8.0 %fusion.136 = (f32[3,640]{1,0:T(4,128)S(1)}, f32[3,640,2176]{2,1,0:T(8,128)}) fusion(pred[640,2176]{1,0:T(8,128)(4,1)S(1)} %fusion.135, bf16[640,3,64]{0,2,1:T(8,128)(2,1)S(1)} %bitcast.146, bf16[2176,3,64]{0,2,1:T(8,128)(2,1)S(1)} %bitcast.145), kind=kOutput, calls=%fused_computation.7.clone.1 | convolution fusion | flops 547305600 | bytes 19193344 | tf_op jit(solution)/shard_map/while/body/eval_jaxpr/qhd,khd->hqk/dot_general | solution.py:146
  245.5 10.5 %fusion.137 = f32[3,640]{1,0:T(4,128)S(1)} fusion(f32[3,640,2176]{2,1,0:T(8,128)} %get-tuple-element.566, f32[3,640]{1,0:T(4,128)S(1)} %get-tuple-element.567, pred[640,2176]{1,0:T(8,128)(4,1)S(1)} %fusion.135), kind=kLoop, calls=%fused_computation.8.clone.1 | loop fusion | flops 16709760 | bytes 18119680 | tf_op jit(solution)/shard_map/while/body/eval_jaxpr/reduce_sum | solution.py:155
  256.0 8.9 %fusion.138 = bf16[3,64,640]{2,1,0:T(8,128)(2,1)S(1)} fusion(bf16[2176,3,64]{0,2,1:T(8,128)(2,1)S(1)} %bitcast.144, f32[3,640,2176]{2,1,0:T(8,128)} %get-tuple-element.566, f32[3,640]{1,0:T(4,128)S(1)} %fusion.137, f32[3,640]{1,0:T(4,128)S(1)} %get-tuple-element.567, pred[640,2176]{1,0:T(8,128)(4,1)S(1)} %fusion.135), kind=kOutput, calls=%fused_computation.15.clone.1 | convolution fusion | flops 555786240 | bytes 19201024 | tf_op jit(solution)/shard_map/while/body/eval_jaxpr/hqk,khd->qhd/dot_general | solution.py:157
  271.0 32.7 %reduce-scatter.5.cloned.1.call-done = bf16[320,768]{1,0:T(8,128)(2,1)} async-done(((bf16[1280,768]{1,0:T(8,128)(2,1)}), bf16[320,768]{1,0:T(8,128)(2,1)}) %reduce-scatter.5.cloned.1.call-update) | async-done | bytes 491536 | tf_op jit(solution)/shard_map/reduce_scatter | solution.py:165
  308.4 8.9 %all-gather.11.cloned.1.call-done = bf16[768,768]{1,0:T(8,128)(2,1)} async-done(((bf16[96,768]{1,0:T(8,128)(2,1)}), bf16[768,768]{1,0:T(8,128)(2,1)}) %all-gather.11.cloned.1.call-update) | async-done | bytes 1179664 | tf_op jit(solution)/shard_map/all_gather | solution.py:82
  317.4 22.3 %all-gather.9.cloned.1.call-done = bf16[1280,768]{1,0:T(8,128)(2,1)} async-done(((bf16[320,768]{1,0:T(8,128)(2,1)}), bf16[1280,768]{1,0:T(8,128)(2,1)}) %all-gather.9.cloned.1.call-update) | async-done | bytes 1966096 | tf_op jit(solution)/shard_map/all_gather | solution.py:174
  339.7 5.5 fusion.64
  345.1 38.4 %all-gather.13.cloned.1.call-done = bf16[768,768]{0,1:T(8,128)(2,1)} async-done(((bf16[768,96]{0,1:T(8,128)(2,1)}), bf16[768,768]{0,1:T(8,128)(2,1)}) %all-gather.13.cloned.1.call-update) | async-done | bytes 1179664 | tf_op jit(solution)/shard_map/all_gather | solution.py:83
  383.5 21.9 %all-gather.15.cloned.1.call-done = bf16[1280,768]{1,0:T(8,128)(2,1)} async-done(((bf16[320,768]{1,0:T(8,128)(2,1)}), bf16[1280,768]{1,0:T(8,128)(2,1)}) %all-gather.15.cloned.1.call-update) | async-done | bytes 1966096 | tf_op jit(solution)/shard_map/all_gather | solution.py:184
  405.4 13.1 %add_convert_fusion = (bf16[1280,768]{1,0:T(8,128)(2,1)S(1)}, f32[1280,768]{1,0:T(8,128)}) fusion(f32[1280,768]{1,0:T(8,128)} %fusion.64, bf16[1280,768]{1,0:T(8,128)(2,1)} %all-gather.15.cloned.1.call-done, bf16[768,768]{0,1:T(8,128)(2,1)} %all-gather.13.cloned.1.call-done), kind=kOutput, calls=%fused_computation.47 | convolution fusion | flops 1580728320 | bytes 12976128 | tf_op jit(solution)/shard_map/td,fd->tf/dot_general | solution.py:186
  419.8 4.4 convolution_convert_fusion.1
  424.3 30.7 %reduce-scatter.9.cloned.1.call-done = bf16[320,768]{1,0:T(8,128)(2,1)} async-done(((bf16[1280,768]{1,0:T(8,128)(2,1)}), bf16[320,768]{1,0:T(8,128)(2,1)}) %reduce-scatter.9.cloned.1.call-update) | async-done | bytes 491536 | tf_op jit(solution)/shard_map/reduce_scatter | solution.py:194
  459.9 21.4 %all-gather.17.cloned.1.call-done = bf16[1280,768]{1,0:T(8,128)(2,1)} async-done(((bf16[320,768]{1,0:T(8,128)(2,1)}), bf16[1280,768]{1,0:T(8,128)(2,1)}) %all-gather.17.cloned.1.call-update) | async-done | bytes 1966096 | tf_op jit(solution)/shard_map/all_gather | solution.py:204
  487.6 112.6 %while.30 = (s32[]{:T(128)}, bf16[1280,192]{0,1:T(8,128)(2,1)}, f32[2816,384]{0,1:T(8,128)}, bf16[2816,384]{0,1:T(8,128)(2,1)}, s32[2816]{0:T(1024)S(1)}, /*inde...) while((s32[]{:T(128)}, bf16[1280,192]{0,1:T(8,128)(2,1)}, ...), condition=%wide.region_14.15_spmd.clone, body=%wide.region_12.14_spmd.clone.sunk | while | flops 2727729920 | bytes 220916592 | solution.py:253
  488.9 4.8 fusion.151
  495.2 8.1 %fusion.150 = f32[3,640,2176]{2,1,0:T(8,128)} fusion(bf16[640,3,64]{0,2,1:T(8,128)(2,1)S(1)} %bitcast.141, bf16[2176,3,64]{0,2,1:T(8,128)(2,1)S(1)} %bitcast.140), kind=kOutput, calls=%fused_computation.138.clone.1 | convolution fusion | flops 534773760 | bytes 17793024 | tf_op jit(solution)/shard_map/while/body/eval_jaxpr/qhd,khd->hqk/dot_general | solution.py:219
  503.3 15.1 %multiply_reduce_fusion.3 = (f32[3,640]{1,0:T(4,128)S(1)}, f32[3,640,2176]{2,1,0:T(8,128)}) fusion(f32[3,640,2176]{2,1,0:T(8,128)} %fusion.150, f32[3,640]{1,0:T(4,128)S(1)} %dynamic-slice_bitcast_fusion.2, bf16[640,3,64]{0,2,1:T(8,128)(2,1)S(1)} %bitcast.138, bf16[2176,3,64]{0,2,1:T(8,128)(2,1)S(1)} %bitcast.135, pred[640,2176]{1,0:T(8,128)(4,1)S(1)} %fusion.151), kind=kOutput, calls=%fused_computation.24.clone.1 | convolution fusion | flops 555661440 | bytes 35912704 | tf_op jit(solution)/shard_map/while/body/eval_jaxpr/qhd,khd->hqk/dot_general | solution.py:146
  518.5 11.4 %multiply_convert_fusion.4 = bf16[3,640,2176]{2,1,0:T(8,128)(2,1)S(1)} fusion(f32[3,640,2176]{2,1,0:T(8,128)} %get-tuple-element.583, f32[3,640,2176]{2,1,0:T(8,128)} %fusion.150, f32[3,640]{1,0:T(4,128)S(1)} %get-tuple-element.584), kind=kLoop, calls=%fused_computation.23.clone.1 | loop fusion | flops 12533760 | bytes 41786880 | tf_op jit(solution)/shard_map/while/body/eval_jaxpr/convert_element_type | solution.py:223
  529.9 3.9 copy-done
  539.5 4.4 fusion.153
  545.1 4.8 fusion.151
  551.5 8.1 %fusion.150 = f32[3,640,2176]{2,1,0:T(8,128)} fusion(bf16[640,3,64]{0,2,1:T(8,128)(2,1)S(1)} %bitcast.141, bf16[2176,3,64]{0,2,1:T(8,128)(2,1)S(1)} %bitcast.140), kind=kOutput, calls=%fused_computation.138.clone.1 | convolution fusion | flops 534773760 | bytes 17793024 | tf_op jit(solution)/shard_map/while/body/eval_jaxpr/qhd,khd->hqk/dot_general | solution.py:219
  559.6 15.1 %multiply_reduce_fusion.3 = (f32[3,640]{1,0:T(4,128)S(1)}, f32[3,640,2176]{2,1,0:T(8,128)}) fusion(f32[3,640,2176]{2,1,0:T(8,128)} %fusion.150, f32[3,640]{1,0:T(4,128)S(1)} %dynamic-slice_bitcast_fusion.2, bf16[640,3,64]{0,2,1:T(8,128)(2,1)S(1)} %bitcast.138, bf16[2176,3,64]{0,2,1:T(8,128)(2,1)S(1)} %bitcast.135, pred[640,2176]{1,0:T(8,128)(4,1)S(1)} %fusion.151), kind=kOutput, calls=%fused_computation.24.clone.1 | convolution fusion | flops 555661440 | bytes 35912704 | tf_op jit(solution)/shard_map/while/body/eval_jaxpr/qhd,khd->hqk/dot_general | solution.py:146
  574.7 11.4 %multiply_convert_fusion.4 = bf16[3,640,2176]{2,1,0:T(8,128)(2,1)S(1)} fusion(f32[3,640,2176]{2,1,0:T(8,128)} %get-tuple-element.583, f32[3,640,2176]{2,1,0:T(8,128)} %fusion.150, f32[3,640]{1,0:T(4,128)S(1)} %get-tuple-element.584), kind=kLoop, calls=%fused_computation.23.clone.1 | loop fusion | flops 12533760 | bytes 41786880 | tf_op jit(solution)/shard_map/while/body/eval_jaxpr/convert_element_type | solution.py:223
  586.1 3.9 copy-done
  595.7 4.4 fusion.153
  606.3 27.3 %collective-permute-done.3 = bf16[256,384]{0,1:T(8,128)(2,1)S(1)} collective-permute-done((bf16[256,384]{0,1:T(8,128)(2,1)S(1)}, bf16[256,384]{0,1:T(8,128)(2,1)S(1)}, u32[]{:S(2)}, u32[]{:S(2)}) %collective-permute-start.3) | collective-permute-done | bytes 196640 | tf_op jit(solution)/shard_map/ppermute | solution.py:16
  638.9 4.0 multiply_convert_fusion.1
  645.7 4.3 all-to-all-start.3
  650.0 4.3 convolution_convert_fusion.2
  667.0 11.4 %all-to-all-done.3 = bf16[8,768,96]{1,2,0:T(8,128)(2,1)} async-done(((bf16[8,768,96]{1,2,0:T(8,128)(2,1)}), bf16[8,768,96]{1,2,0:T(8,128)(2,1)}, u32[]{:S(2)}, u32[]{:S(2)}) %all-to-all-start.3) | async-done | bytes 1179680 | tf_op jit(solution)/shard_map/all_to_all | solution.py:27
  678.4 4.1 all-to-all-start.1
  686.5 6.5 all-reduce.4
  696.0 6.1 all-to-all-start
  702.2 4.9 convolution_convert_fusion.8
  710.6 15.5 %all-to-all-done = bf16[8,96,577]{2,1,0:T(8,128)(2,1)S(1)} async-done(((bf16[8,96,577]{2,1,0:T(8,128)(2,1)}), bf16[8,96,577]{2,1,0:T(8,128)(2,1)S(1)}, u32[]{:S(2)}, u32[]{:S(2)}) %all-to-all-start) | async-done | bytes 886304 | tf_op jit(solution)/shard_map/all_to_all | solution.py:27
  739.1 24.3 %all-to-all-done.2 = bf16[8,96,769]{2,1,0:T(8,128)(2,1)S(1)} async-done(((bf16[8,96,769]{2,1,0:T(8,128)(2,1)}), bf16[8,96,769]{2,1,0:T(8,128)(2,1)S(1)}, u32[]{:S(2)}, u32[]{:S(2)}) %all-to-all-start.2) | async-done | bytes 1181216 | tf_op jit(solution)/shard_map/all_to_all | solution.py:27
  (242 shorter events, 119.0 us)
Async XLA Ops:
  8.0 95.4 %all-gather.7.cloned.1.call-start = ((), (), s32[]{:S(2)}) async-start(), calls=%async_computation.8 | async-start | bytes 2457600 | tf_op jit(solution)/shard_map/all_gather | solution.py:101
  9.3 30.9 %copy-start.36 = (f32[320]{0:T(512)}, f32[320]{0:T(512)S(1)}, u32[]{:S(2)}) copy-start(f32[320]{0:T(512)S(1)} %add_rsqrt_fusion.1) | copy-start | bytes 3844
  39.2 264.5 %reduce-scatter.5.cloned.1.call-start = ((), (), s32[]{:S(2)}) async-start(), calls=%async_computation.9 | async-start | bytes 2457600 | tf_op jit(solution)/shard_map/reduce_scatter | solution.py:165
  72.2 36.3 %copy-start.19 = (bf16[768,192]{1,0:T(8,128)(2,1)}, bf16[768,192]{1,0:T(8,128)(2,1)S(1)}, u32[]{:S(2)}) copy-start(bf16[768,192]{1,0:T(8,128)(2,1)S(1)} %all_gather.38) | copy-start | bytes 884740
  103.4 52.9 %copy-start.21 = (bf16[768,192]{1,0:T(8,128)(2,1)}, bf16[768,192]{1,0:T(8,128)(2,1)S(1)}, u32[]{:S(2)}) copy-start(bf16[768,192]{1,0:T(8,128)(2,1)S(1)} %all_gather.39) | copy-start | bytes 884740
  103.4 6.6 copy-start.42
  103.4 52.9 %copy-start.35 = (bf16[96,192]{1,0:T(8,128)(2,1)S(1)}, bf16[96,192]{1,0:T(8,128)(2,1)}, u32[]{:S(2)}) copy-start(bf16[96,192]{1,0:T(8,128)(2,1)} %param.21) | copy-start | bytes 110596
  105.9 82.6 %copy-start.3 = (bf16[1280,768]{1,0:T(8,128)(2,1)S(1)}, bf16[1280,768]{1,0:T(8,128)(2,1)}, u32[]{:S(2)}) copy-start(bf16[1280,768]{1,0:T(8,128)(2,1)} %all-gather.7.cloned.1.call-done) | copy-start | bytes 5898244
  108.5 83.2 %collective-permute-start.1 = (bf16[1280,384]{0,1:T(8,128)(2,1)S(1)}, bf16[1280,384]{0,1:T(8,128)(2,1)S(1)}, u32[]{:S(2)}, u32[]{:S(2)}) collective-permute-start(bf16[1280,384]{0,1:T(8,128)(2,1)S(1)} %pad_maximum_fusion.1), channel_id=1, source_target_pairs={{0,4},{4,8},{8,12},{12,16},{16,20},{20,24},{24,28},{1,5},{5,9},{9,... | collective-permute-start | bytes 2949128 | tf_op jit(solution)/shard_map/ppermute | solution.py:16
  187.2 4.5 collective-permute-start
  219.8 8.9 %copy-start.26 = (bf16[2,640,192]{1,2,0:T(8,128)(2,1)S(1)}, bf16[2,640,192]{1,2,0:T(8,128)(2,1)}, u32[]{:S(2)}) copy-start(bf16[2,640,192]{1,2,0:T(8,128)(2,1)} %get-tuple-element.602) | copy-start | bytes 1474564 | tf_op jit(solution)/shard_map/while
  256.0 8.9 %copy-start.26 = (bf16[2,640,192]{1,2,0:T(8,128)(2,1)S(1)}, bf16[2,640,192]{1,2,0:T(8,128)(2,1)}, u32[]{:S(2)}) copy-start(bf16[2,640,192]{1,2,0:T(8,128)(2,1)} %get-tuple-element.602) | copy-start | bytes 1474564 | tf_op jit(solution)/shard_map/while
  265.7 38.0 %copy-start.1 = (bf16[320,768]{1,0:T(8,128)(2,1)S(1)}, bf16[320,768]{1,0:T(8,128)(2,1)}, u32[]{:S(2)}) copy-start(bf16[320,768]{1,0:T(8,128)(2,1)} %param.16) | copy-start | bytes 1474564
  266.9 40.2 %copy-start.10 = (bf16[2,24,8,640]{3,2,0,1:T(8,128)(2,1)}, bf16[2,24,8,640]{3,2,0,1:T(8,128)(2,1)S(1)}, u32[]{:S(2)}) copy-start(bf16[2,24,8,640]{3,2,0,1:T(8,128)(2,1)S(1)} %copy.67) | copy-start | bytes 1474564
  270.1 47.3 %all-gather.11.cloned.1.call-start = ((), (), s32[]{:S(2)}) async-start(), calls=%async_computation.11 | async-start | bytes 1327104 | tf_op jit(solution)/shard_map/all_gather | solution.py:82
  270.7 69.0 %all-gather.9.cloned.1.call-start = ((), (), s32[]{:S(2)}) async-start(), calls=%async_computation.10 | async-start | bytes 2457600 | tf_op jit(solution)/shard_map/all_gather | solution.py:174
  271.0 186.2 %copy-start.29 = (f32[768]{0:T(1024)}, f32[768]{0:T(1024)S(1)}, u32[]{:S(2)}) copy-start(f32[768]{0:T(1024)S(1)} %convert_element_type.159) | copy-start | bytes 9220
  305.0 152.2 %copy-start.33 = (f32[320]{0:T(512)}, f32[320]{0:T(512)S(1)}, u32[]{:S(2)}) copy-start(f32[320]{0:T(512)S(1)} %add_rsqrt_fusion) | copy-start | bytes 3844
  307.1 76.4 %all-gather.13.cloned.1.call-start = ((), (), s32[]{:S(2)}) async-start(), calls=%async_computation.12 | async-start | bytes 1327104 | tf_op jit(solution)/shard_map/all_gather | solution.py:83
  307.6 97.7 %all-gather.15.cloned.1.call-start = ((), (), s32[]{:S(2)}) async-start(), calls=%async_computation.14 | async-start | bytes 2457600 | tf_op jit(solution)/shard_map/all_gather | solution.py:184
  308.4 146.7 %reduce-scatter.9.cloned.1.call-start = ((), (), s32[]{:S(2)}) async-start(), calls=%async_computation.15 | async-start | bytes 2457600 | tf_op jit(solution)/shard_map/reduce_scatter | solution.py:194
  419.8 35.2 %copy-start.5 = (bf16[320,768]{1,0:T(8,128)(2,1)S(1)}, bf16[320,768]{1,0:T(8,128)(2,1)}, u32[]{:S(2)}) copy-start(bf16[320,768]{1,0:T(8,128)(2,1)} %reduce-scatter.5.cloned.1.call-done) | copy-start | bytes 1474564
  419.8 37.4 %copy-start.7 = (bf16[320,768]{1,0:T(8,128)(2,1)S(1)}, bf16[320,768]{1,0:T(8,128)(2,1)}, u32[]{:S(2)}) copy-start(bf16[320,768]{1,0:T(8,128)(2,1)} %param.17) | copy-start | bytes 1474564
  424.2 57.0 %copy-start.25 = (bf16[192,768]{0,1:T(8,128)(2,1)S(1)}, bf16[192,768]{0,1:T(8,128)(2,1)}, u32[]{:S(2)}) copy-start(bf16[192,768]{0,1:T(8,128)(2,1)} %all_gather.41) | copy-start | bytes 884740
  424.2 57.0 %all-gather.17.cloned.1.call-start = ((), (), s32[]{:S(2)}) async-start(), calls=%async_computation.16 | async-start | bytes 2457600 | tf_op jit(solution)/shard_map/all_gather | solution.py:204
  457.2 30.4 %copy-start.38 = (f32[320]{0:T(512)}, f32[320]{0:T(512)S(1)}, u32[]{:S(2)}) copy-start(f32[320]{0:T(512)S(1)} %broadcast_multiply_fusion.1) | copy-start | bytes 3844
  459.4 225.5 %reduce-scatter.11.cloned.1.call-start = ((), (), s32[]{:S(2)}) async-start(), calls=%async_computation.17 | async-start | bytes 2457600 | tf_op jit(solution)/shard_map/reduce_scatter | solution.py:278
  518.5 15.3 %copy-start = (f32[3,640,2176]{2,1,0:T(8,128)S(1)}, f32[3,640,2176]{2,1,0:T(8,128)}, u32[]{:S(2)}) copy-start(f32[3,640,2176]{2,1,0:T(8,128)} %get-tuple-element.583) | copy-start | bytes 50135044 | tf_op jit(solution)/shard_map/while
  574.7 15.3 %copy-start = (f32[3,640,2176]{2,1,0:T(8,128)S(1)}, f32[3,640,2176]{2,1,0:T(8,128)}, u32[]{:S(2)}) copy-start(f32[3,640,2176]{2,1,0:T(8,128)} %get-tuple-element.583) | copy-start | bytes 50135044 | tf_op jit(solution)/shard_map/while
  602.8 30.9 %collective-permute-start.2 = (bf16[1280,384]{0,1:T(8,128)(2,1)S(1)}, bf16[1280,384]{0,1:T(8,128)(2,1)S(1)}, u32[]{:S(2)}, u32[]{:S(2)}) collective-permute-start(bf16[1280,384]{0,1:T(8,128)(2,1)S(1)} %slice.58), channel_id=1, source_target_pairs={{4,0},{8,4},{12,8},{16,12},{20,16},{24,20},{28,24},{5,1},{9,5},{13... | collective-permute-start | bytes 2949128 | tf_op jit(solution)/shard_map/ppermute | solution.py:16
  604.3 29.4 %collective-permute-start.3 = (bf16[256,384]{0,1:T(8,128)(2,1)S(1)}, bf16[256,384]{0,1:T(8,128)(2,1)S(1)}, u32[]{:S(2)}, u32[]{:S(2)}) collective-permute-start(bf16[256,384]{0,1:T(8,128)(2,1)S(1)} %slice.59), channel_id=1, source_target_pairs={{8,0},{12,4},{16,8},{20,12},{24,16},{28,20},{9,1},{13,5},{17,9},{2... | collective-permute-start | bytes 589832 | tf_op jit(solution)/shard_map/ppermute | solution.py:16
  605.6 29.9 %copy-start.20 = (bf16[768,192]{1,0:T(8,128)(2,1)S(1)}, bf16[768,192]{1,0:T(8,128)(2,1)}, u32[]{:S(2)}) copy-start(bf16[768,192]{1,0:T(8,128)(2,1)} %copy-done.19) | copy-start | bytes 884740
  645.7 32.7 %all-to-all-start.3 = ((bf16[8,768,96]{1,2,0:T(8,128)(2,1)}), bf16[8,768,96]{1,2,0:T(8,128)(2,1)}, u32[]{:S(2)}, u32[]{:S(2)}) async-start(bf16[8,768,96]{1,2,0:T(8,128)(2,1)} %bitcast.154), calls=%async_computation.7 | async-start | bytes 2359296 | tf_op jit(solution)/shard_map/all_to_all | solution.py:27
  650.0 84.5 %reduce-scatter.7.cloned.1.call-start = ((), (), s32[]{:S(2)}) async-start(), calls=%async_computation.13 | async-start | bytes 2457600 | tf_op jit(solution)/shard_map/reduce_scatter | solution.py:177
  658.6 23.9 %copy-start.18 = (bf16[1280,384]{0,1:T(8,128)(2,1)S(1)}, bf16[1280,384]{0,1:T(8,128)(2,1)}, u32[]{:S(2)}) copy-start(bf16[1280,384]{0,1:T(8,128)(2,1)} %copy-done.17) | copy-start | bytes 2949124
  662.8 22.2 %copy-start.2 = (bf16[320,768]{1,0:T(8,128)(2,1)S(1)}, bf16[320,768]{1,0:T(8,128)(2,1)}, u32[]{:S(2)}) copy-start(bf16[320,768]{1,0:T(8,128)(2,1)} %param.16) | copy-start | bytes 1474564
  662.8 22.2 %copy-start.32 = (f32[768]{0:T(1024)S(1)}, f32[768]{0:T(1024)}, u32[]{:S(2)}) copy-start(f32[768]{0:T(1024)} %copy-done.31) | copy-start | bytes 9220
  662.8 22.2 %copy-start.37 = (f32[320]{0:T(512)S(1)}, f32[320]{0:T(512)}, u32[]{:S(2)}) copy-start(f32[320]{0:T(512)} %copy-done.36) | copy-start | bytes 3844
  662.8 23.7 %copy-start.40 = (f32[768]{0:T(1024)S(1)}, f32[768]{0:T(1024)}, u32[]{:S(2)}) copy-start(f32[768]{0:T(1024)} %get-tuple-element.370) | copy-start | bytes 9220
  678.4 17.6 %all-to-all-start.1 = ((bf16[8,192,96]{2,1,0:T(8,128)(2,1)}), bf16[8,192,96]{2,1,0:T(8,128)(2,1)}, u32[]{:S(2)}, u32[]{:S(2)}) async-start(bf16[8,192,96]{2,1,0:T(8,128)(2,1)} %bitcast.150), calls=%async_computation.5 | async-start | bytes 786432 | tf_op jit(solution)/shard_map/all_to_all | solution.py:27
  696.0 30.0 %all-to-all-start = ((bf16[8,96,577]{2,1,0:T(8,128)(2,1)}), bf16[8,96,577]{2,1,0:T(8,128)(2,1)S(1)}, u32[]{:S(2)}, u32[]{:S(2)}) async-start(bf16[8,96,577]{2,1,0:T(8,128)(2,1)} %pad_maximum_fusion.2), calls=%async_computation.4 | async-start | bytes 1966080 | tf_op jit(solution)/shard_map/all_to_all | solution.py:27
  707.1 27.4 %copy-start.6 = (bf16[320,768]{1,0:T(8,128)(2,1)S(1)}, bf16[320,768]{1,0:T(8,128)(2,1)}, u32[]{:S(2)}) copy-start(bf16[320,768]{1,0:T(8,128)(2,1)} %reduce-scatter.5.cloned.1.call-done) | copy-start | bytes 1474564
  707.1 27.4 %copy-start.8 = (bf16[320,768]{1,0:T(8,128)(2,1)S(1)}, bf16[320,768]{1,0:T(8,128)(2,1)}, u32[]{:S(2)}) copy-start(bf16[320,768]{1,0:T(8,128)(2,1)} %param.17) | copy-start | bytes 1474564
  707.1 27.4 %copy-start.9 = (bf16[320,768]{1,0:T(8,128)(2,1)S(1)}, bf16[320,768]{1,0:T(8,128)(2,1)}, u32[]{:S(2)}) copy-start(bf16[320,768]{1,0:T(8,128)(2,1)} %reduce-scatter.9.cloned.1.call-done) | copy-start | bytes 1474564
  707.1 27.4 %copy-start.30 = (f32[768]{0:T(1024)S(1)}, f32[768]{0:T(1024)}, u32[]{:S(2)}) copy-start(f32[768]{0:T(1024)} %copy-done.29) | copy-start | bytes 9220
  707.1 27.4 %copy-start.34 = (f32[320]{0:T(512)S(1)}, f32[320]{0:T(512)}, u32[]{:S(2)}) copy-start(f32[320]{0:T(512)} %copy-done.33) | copy-start | bytes 3844
  707.1 27.4 %copy-start.39 = (f32[320]{0:T(512)S(1)}, f32[320]{0:T(512)}, u32[]{:S(2)}) copy-start(f32[320]{0:T(512)} %copy-done.38) | copy-start | bytes 3844
  727.0 36.4 %all-to-all-start.2 = ((bf16[8,96,769]{2,1,0:T(8,128)(2,1)}), bf16[8,96,769]{2,1,0:T(8,128)(2,1)S(1)}, u32[]{:S(2)}, u32[]{:S(2)}) async-start(bf16[8,96,769]{2,1,0:T(8,128)(2,1)} %pad_maximum_fusion), calls=%async_computation.6 | async-start | bytes 2752512 | tf_op jit(solution)/shard_map/all_to_all | solution.py:27
  (20 other events, 61.3 us)
Sparse Core Ops, SparseCore 0:
  39.3 19.0 all-gather.6
  270.2 33.4 reduce-scatter.4
  424.4 30.6 reduce-scatter.8
  639.0 28.7 reduce-scatter.10
  670.4 30.8 reduce-scatter.6
Sparse Core Ops, SparseCore 1:
  273.0 44.3 all-gather.10
  319.5 20.1 all-gather.8
  342.0 41.5 all-gather.12
  385.2 20.1 all-gather.14
  459.5 21.7 all-gather.16
where the time goes:
time: 778 us; the launch traced here: 773 us
  waiting for transfers between devices  259 us (33%)
  blocking collectives  170 us (22%)
  matrix products  150 us (19%)
  other arithmetic  107 us (14%)
  local copies, waits for them, and re-layouts  43.4 us (6%)
  starting transfers between devices  24.5 us (3%)
  between operations  17 us (2%)
    all_to_all x4, waiting for transfers between devices, sum_at_owner(): lax.all_to_all(tiles, axis, split_axis=0, concat_axis=0, tiled=True)  51.2 us
    dot_general x4, matrix products, scores_of(): jnp.einsum('qhd,khd->hqk', query_block, key_block, preferred_element_type...  46.3 us
    all_gather x1, blocking collectives, shards(): lax.all_gather(w_out, 'dp', axis=1, tiled=True)  46 us
    all_gather x1, waiting for transfers between devices, shards(): lax.all_gather(w_down, 'dp', axis=1, tiled=True)  38.4 us
    reduce_scatter x1, waiting for transfers between devices, shards(): lax.psum_scatter(jnp.dot(context, full_out, preferred_element_type=jnp.fl...  32.7 us
    all_gather x1, blocking collectives, shards(): lax.all_gather(w_key, 'dp', axis=0, tiled=True)  31.2 us
    all_gather x1, blocking collectives, shards(): lax.all_gather(w_value, 'dp', axis=0, tiled=True)  31.2 us
    all_gather x1, blocking collectives, shards(): lax.all_gather(w_query, 'dp', axis=0, tiled=True)  31 us
  transfers between devices with their start and end apart: 18, of which 12 were waited for; matrix products, arithmetic and copies ran while one was open for 8% of the time, Pallas kernels for 0%

commit v1 on v0

--- a/solution.py
+++ b/solution.py
@@ -201,7 +201,12 @@
     ).astype(jnp.float32)
     through_two, gain_two_part = norm_backward(grad_normed_two, hat_two, factor_two, gain_two)
     grad_middle = incoming + through_two
-    grad_middle_all = lax.all_gather(grad_middle.astype(jnp.bfloat16), "tensor", axis=0, tiled=True)
+    grad_middle_all = jnp.concatenate(
+        lax.all_to_all(
+            jnp.stack([grad_middle.astype(jnp.bfloat16)] * lax.axis_size("tensor")), "tensor", 0, 0
+        ),
+        axis=0,
+    )
     grad_out = jnp.einsum("tc,td->cd", context, grad_middle_all, preferred_element_type=jnp.float32)
     grad_context = jnp.einsum(
         "td,cd->tc", grad_middle_all, full_out, preferred_element_type=jnp.float32

time: 778 us -> 782 us (level)
    all_to_all x0 -> x1, waiting for transfers between devices: none -> 23.8 us  [shards(): lax.all_to_all(jnp.stack([grad_middle.astype(jnp.bfloat16)] * lax.axis_si...]
    all_gather x1 -> x0, waiting for transfers between devices: 21.4 us -> none  [shards(): lax.all_gather(grad_middle.astype(jnp.bfloat16), 'tensor', axis=0, tiled=...]
where the time goes in v1:
time: 782 us; the launch traced here: 776 us
  waiting for transfers between devices  260 us (33%)
  blocking collectives  169 us (22%)
  matrix products  148 us (19%)
  other arithmetic  107 us (14%)
  local copies, waits for them, and re-layouts  44.8 us (6%)
  starting transfers between devices  28.1 us (4%)
  between operations  16.7 us (2%)
    all_to_all x4, waiting for transfers between devices, sum_at_owner(): lax.all_to_all(tiles, axis, split_axis=0, concat_axis=0, tiled=True)  50.8 us
    dot_general x4, matrix products, scores_of(): jnp.einsum('qhd,khd->hqk', query_block, key_block, preferred_element_type...  46.3 us
    all_gather x1, blocking collectives, shards(): lax.all_gather(w_out, 'dp', axis=1, tiled=True)  46 us
    all_gather x1, waiting for transfers between devices, shards(): lax.all_gather(w_down, 'dp', axis=1, tiled=True)  38.4 us
    reduce_scatter x1, waiting for transfers between devices, shards(): lax.psum_scatter(jnp.dot(context, full_out, preferred_element_type=jnp.fl...  32.7 us
    all_gather x1, blocking collectives, shards(): lax.all_gather(w_key, 'dp', axis=0, tiled=True)  31.2 us
    all_gather x1, blocking collectives, shards(): lax.all_gather(w_value, 'dp', axis=0, tiled=True)  31.2 us
    all_gather x1, blocking collectives, shards(): lax.all_gather(w_query, 'dp', axis=0, tiled=True)  31 us
  transfers between devices with their start and end apart: 18, of which 12 were waited for; matrix products, arithmetic and copies ran while one was open for 8% of the time, Pallas kernels for 0%

profile of v1, /device:TPU:0, one launch (start us, length us, event | category | flops | bytes accessed | tf_op | source)
XLA Modules:
  0.0 776.2 jit_solution(7014333604060535724)
XLA Ops:
  12.9 23.7 %all-reduce.5 = (bf16[768]{0:T(1024)(128)(2,1)S(1)}, bf16[768]{0:T(1024)(128)(2,1)}) all-reduce(bf16[768]{0:T(1024)(128)(2,1)S(1)} %dynamic-update-slice, bf16[768]{0:T(1024)(128)(2,1)S(1)} %dynamic-update-slice.1), channel_id=1, replica_groups=mesh['dp'=8,'tensor'=4] {'dp'}, use_global_device_ids=true, to_apply=%add.2 | all-reduce | flops 1536 | bytes 6144
  41.0 31.2 %all_gather.35 = bf16[768,192]{1,0:T(8,128)(2,1)S(1)} all-gather(bf16[96,192]{1,0:T(8,128)(2,1)} %param.22), channel_id=1, replica_groups=mesh['dp'=8,'tensor'=4] {'dp'}, dimensions={0}, use_global_device_ids=true | all-gather | bytes 331776 | tf_op jit(solution)/shard_map/all_gather | solution.py:78
  72.2 31.2 %all_gather.36 = bf16[768,192]{1,0:T(8,128)(2,1)S(1)} all-gather(bf16[96,192]{1,0:T(8,128)(2,1)} %param.23), channel_id=1, replica_groups=mesh['dp'=8,'tensor'=4] {'dp'}, dimensions={0}, use_global_device_ids=true | all-gather | bytes 331776 | tf_op jit(solution)/shard_map/all_gather | solution.py:79
  110.2 46.0 %all_gather.38 = bf16[192,768]{0,1:T(8,128)(2,1)} all-gather(bf16[192,96]{0,1:T(8,128)(2,1)S(1)} %copy.48), channel_id=1, replica_groups=mesh['dp'=8,'tensor'=4] {'dp'}, dimensions={1}, use_global_device_ids=true | all-gather | bytes 331776 | tf_op jit(solution)/shard_map/all_gather | solution.py:80
  156.2 31.0 %all_gather.37 = bf16[768,192]{1,0:T(8,128)(2,1)S(1)} all-gather(bf16[96,192]{1,0:T(8,128)(2,1)S(1)} %copy-done.36), channel_id=1, replica_groups=mesh['dp'=8,'tensor'=4] {'dp'}, dimensions={0}, use_global_device_ids=true | all-gather | bytes 331776 | tf_op jit(solution)/shard_map/all_gather | solution.py:77
  193.2 72.5 %while.29 = (s32[]{:T(128)}, bf16[2,640,192]{1,2,0:T(8,128)(2,1)}, f32[2,3,640]{2,1,0:T(4,128)S(1)}, s32[2]{0:T(128)S(1)}, bf16[2816,384]{0,1:T(8,128)(2,1)}, /*...) while((s32[]{:T(128)}, bf16[2,640,192]{1,2,0:T(8,128)(2,1)}, ...), condition=%wide.region_6.7_spmd.clone, body=%wide.region_3.6_spmd.clone.sunk | while | flops 1133730560 | bytes 66249560 | solution.py:163
  195.0 4.8 fusion.135
  201.3 8.0 %fusion.136 = (f32[3,640]{1,0:T(4,128)S(1)}, f32[3,640,2176]{2,1,0:T(8,128)}) fusion(pred[640,2176]{1,0:T(8,128)(4,1)S(1)} %fusion.135, bf16[640,3,64]{0,2,1:T(8,128)(2,1)S(1)} %bitcast.149, bf16[2176,3,64]{0,2,1:T(8,128)(2,1)S(1)} %bitcast.146), kind=kOutput, calls=%fused_computation.7.clone.1 | convolution fusion | flops 547305600 | bytes 19193344 | tf_op jit(solution)/shard_map/while/body/eval_jaxpr/qhd,khd->hqk/dot_general | solution.py:146
  209.3 10.5 %fusion.137 = f32[3,640]{1,0:T(4,128)S(1)} fusion(f32[3,640,2176]{2,1,0:T(8,128)} %get-tuple-element.566, f32[3,640]{1,0:T(4,128)S(1)} %get-tuple-element.567, pred[640,2176]{1,0:T(8,128)(4,1)S(1)} %fusion.135), kind=kLoop, calls=%fused_computation.8.clone.1 | loop fusion | flops 16709760 | bytes 18119680 | tf_op jit(solution)/shard_map/while/body/eval_jaxpr/reduce_sum | solution.py:155
  219.8 8.8 %fusion.138 = bf16[3,64,640]{2,1,0:T(8,128)(2,1)S(1)} fusion(bf16[2176,3,64]{0,2,1:T(8,128)(2,1)S(1)} %bitcast.145, f32[3,640,2176]{2,1,0:T(8,128)} %get-tuple-element.566, f32[3,640]{1,0:T(4,128)S(1)} %fusion.137, f32[3,640]{1,0:T(4,128)S(1)} %get-tuple-element.567, pred[640,2176]{1,0:T(8,128)(4,1)S(1)} %fusion.135), kind=kOutput, calls=%fused_computation.15.clone.1 | convolution fusion | flops 555786240 | bytes 19201024 | tf_op jit(solution)/shard_map/while/body/eval_jaxpr/hqk,khd->qhd/dot_general | solution.py:157
  231.1 4.8 fusion.135
  237.5 8.0 %fusion.136 = (f32[3,640]{1,0:T(4,128)S(1)}, f32[3,640,2176]{2,1,0:T(8,128)}) fusion(pred[640,2176]{1,0:T(8,128)(4,1)S(1)} %fusion.135, bf16[640,3,64]{0,2,1:T(8,128)(2,1)S(1)} %bitcast.149, bf16[2176,3,64]{0,2,1:T(8,128)(2,1)S(1)} %bitcast.146), kind=kOutput, calls=%fused_computation.7.clone.1 | convolution fusion | flops 547305600 | bytes 19193344 | tf_op jit(solution)/shard_map/while/body/eval_jaxpr/qhd,khd->hqk/dot_general | solution.py:146
  245.5 10.5 %fusion.137 = f32[3,640]{1,0:T(4,128)S(1)} fusion(f32[3,640,2176]{2,1,0:T(8,128)} %get-tuple-element.566, f32[3,640]{1,0:T(4,128)S(1)} %get-tuple-element.567, pred[640,2176]{1,0:T(8,128)(4,1)S(1)} %fusion.135), kind=kLoop, calls=%fused_computation.8.clone.1 | loop fusion | flops 16709760 | bytes 18119680 | tf_op jit(solution)/shard_map/while/body/eval_jaxpr/reduce_sum | solution.py:155
  256.0 8.9 %fusion.138 = bf16[3,64,640]{2,1,0:T(8,128)(2,1)S(1)} fusion(bf16[2176,3,64]{0,2,1:T(8,128)(2,1)S(1)} %bitcast.145, f32[3,640,2176]{2,1,0:T(8,128)} %get-tuple-element.566, f32[3,640]{1,0:T(4,128)S(1)} %fusion.137, f32[3,640]{1,0:T(4,128)S(1)} %get-tuple-element.567, pred[640,2176]{1,0:T(8,128)(4,1)S(1)} %fusion.135), kind=kOutput, calls=%fused_computation.15.clone.1 | convolution fusion | flops 555786240 | bytes 19201024 | tf_op jit(solution)/shard_map/while/body/eval_jaxpr/hqk,khd->qhd/dot_general | solution.py:157
  271.0 32.7 %reduce-scatter.5.cloned.1.call-done = bf16[320,768]{1,0:T(8,128)(2,1)} async-done(((bf16[1280,768]{1,0:T(8,128)(2,1)}), bf16[320,768]{1,0:T(8,128)(2,1)}) %reduce-scatter.5.cloned.1.call-update) | async-done | bytes 491536 | tf_op jit(solution)/shard_map/reduce_scatter | solution.py:165
  308.4 8.7 %all-gather.10.cloned.1.call-done = bf16[768,768]{1,0:T(8,128)(2,1)} async-done(((bf16[96,768]{1,0:T(8,128)(2,1)}), bf16[768,768]{1,0:T(8,128)(2,1)}) %all-gather.10.cloned.1.call-update) | async-done | bytes 1179664 | tf_op jit(solution)/shard_map/all_gather | solution.py:82
  317.1 22.3 %all-gather.8.cloned.1.call-done = bf16[1280,768]{1,0:T(8,128)(2,1)} async-done(((bf16[320,768]{1,0:T(8,128)(2,1)}), bf16[1280,768]{1,0:T(8,128)(2,1)}) %all-gather.8.cloned.1.call-update) | async-done | bytes 1966096 | tf_op jit(solution)/shard_map/all_gather | solution.py:174
  339.4 5.5 fusion.64
  344.9 38.4 %all-gather.12.cloned.1.call-done = bf16[768,768]{0,1:T(8,128)(2,1)} async-done(((bf16[768,96]{0,1:T(8,128)(2,1)}), bf16[768,768]{0,1:T(8,128)(2,1)}) %all-gather.12.cloned.1.call-update) | async-done | bytes 1179664 | tf_op jit(solution)/shard_map/all_gather | solution.py:83
  383.3 21.9 %all-gather.14.cloned.1.call-done = bf16[1280,768]{1,0:T(8,128)(2,1)} async-done(((bf16[320,768]{1,0:T(8,128)(2,1)}), bf16[1280,768]{1,0:T(8,128)(2,1)}) %all-gather.14.cloned.1.call-update) | async-done | bytes 1966096 | tf_op jit(solution)/shard_map/all_gather | solution.py:184
  405.1 13.1 %add_convert_fusion = (bf16[1280,768]{1,0:T(8,128)(2,1)S(1)}, f32[1280,768]{1,0:T(8,128)}) fusion(f32[1280,768]{1,0:T(8,128)} %fusion.64, bf16[1280,768]{1,0:T(8,128)(2,1)} %all-gather.14.cloned.1.call-done, bf16[768,768]{0,1:T(8,128)(2,1)} %all-gather.12.cloned.1.call-done), kind=kOutput, calls=%fused_computation.47 | convolution fusion | flops 1580728320 | bytes 12976128 | tf_op jit(solution)/shard_map/td,fd->tf/dot_general | solution.py:186
  419.6 4.4 convolution_convert_fusion.1
  424.0 30.8 %reduce-scatter.9.cloned.1.call-done = bf16[320,768]{1,0:T(8,128)(2,1)} async-done(((bf16[1280,768]{1,0:T(8,128)(2,1)}), bf16[320,768]{1,0:T(8,128)(2,1)}) %reduce-scatter.9.cloned.1.call-update) | async-done | bytes 491536 | tf_op jit(solution)/shard_map/reduce_scatter | solution.py:194
  463.9 23.8 %all-to-all-done = bf16[4,320,768]{2,1,0:T(8,128)(2,1)S(1)} async-done(((bf16[4,320,768]{2,1,0:T(8,128)(2,1)}), bf16[4,320,768]{2,1,0:T(8,128)(2,1)S(1)}, u32[]{:S(2)}, u32[]{:S(2)}) %all-to-all-start) | async-done | bytes 1966112 | tf_op jit(solution)/shard_map/all_to_all | solution.py:205
  492.5 112.6 %while.30 = (s32[]{:T(128)}, bf16[1280,192]{0,1:T(8,128)(2,1)}, f32[2816,384]{0,1:T(8,128)}, bf16[2816,384]{0,1:T(8,128)(2,1)}, s32[2816]{0:T(1024)S(1)}, /*inde...) while((s32[]{:T(128)}, bf16[1280,192]{0,1:T(8,128)(2,1)}, ...), condition=%wide.region_14.15_spmd.clone, body=%wide.region_12.14_spmd.clone.sunk | while | flops 2727729920 | bytes 220916592 | solution.py:258
  493.8 4.8 fusion.151
  500.2 8.1 %fusion.150 = f32[3,640,2176]{2,1,0:T(8,128)} fusion(bf16[640,3,64]{0,2,1:T(8,128)(2,1)S(1)} %bitcast.142, bf16[2176,3,64]{0,2,1:T(8,128)(2,1)S(1)} %bitcast.141), kind=kOutput, calls=%fused_computation.138.clone.1 | convolution fusion | flops 534773760 | bytes 17793024 | tf_op jit(solution)/shard_map/while/body/eval_jaxpr/qhd,khd->hqk/dot_general | solution.py:224
  508.3 15.1 %multiply_reduce_fusion.3 = (f32[3,640]{1,0:T(4,128)S(1)}, f32[3,640,2176]{2,1,0:T(8,128)}) fusion(f32[3,640,2176]{2,1,0:T(8,128)} %fusion.150, f32[3,640]{1,0:T(4,128)S(1)} %dynamic-slice_bitcast_fusion.2, bf16[640,3,64]{0,2,1:T(8,128)(2,1)S(1)} %bitcast.139, bf16[2176,3,64]{0,2,1:T(8,128)(2,1)S(1)} %bitcast.136, pred[640,2176]{1,0:T(8,128)(4,1)S(1)} %fusion.151), kind=kOutput, calls=%fused_computation.24.clone.1 | convolution fusion | flops 555661440 | bytes 35912704 | tf_op jit(solution)/shard_map/while/body/eval_jaxpr/qhd,khd->hqk/dot_general | solution.py:146
  523.4 11.4 %multiply_convert_fusion.4 = bf16[3,640,2176]{2,1,0:T(8,128)(2,1)S(1)} fusion(f32[3,640,2176]{2,1,0:T(8,128)} %get-tuple-element.583, f32[3,640,2176]{2,1,0:T(8,128)} %fusion.150, f32[3,640]{1,0:T(4,128)S(1)} %get-tuple-element.584), kind=kLoop, calls=%fused_computation.23.clone.1 | loop fusion | flops 12533760 | bytes 41786880 | tf_op jit(solution)/shard_map/while/body/eval_jaxpr/convert_element_type | solution.py:228
  534.8 3.9 copy-done
  544.4 4.4 fusion.153
  550.1 4.8 fusion.151
  556.5 8.1 %fusion.150 = f32[3,640,2176]{2,1,0:T(8,128)} fusion(bf16[640,3,64]{0,2,1:T(8,128)(2,1)S(1)} %bitcast.142, bf16[2176,3,64]{0,2,1:T(8,128)(2,1)S(1)} %bitcast.141), kind=kOutput, calls=%fused_computation.138.clone.1 | convolution fusion | flops 534773760 | bytes 17793024 | tf_op jit(solution)/shard_map/while/body/eval_jaxpr/qhd,khd->hqk/dot_general | solution.py:224
  564.5 15.1 %multiply_reduce_fusion.3 = (f32[3,640]{1,0:T(4,128)S(1)}, f32[3,640,2176]{2,1,0:T(8,128)}) fusion(f32[3,640,2176]{2,1,0:T(8,128)} %fusion.150, f32[3,640]{1,0:T(4,128)S(1)} %dynamic-slice_bitcast_fusion.2, bf16[640,3,64]{0,2,1:T(8,128)(2,1)S(1)} %bitcast.139, bf16[2176,3,64]{0,2,1:T(8,128)(2,1)S(1)} %bitcast.136, pred[640,2176]{1,0:T(8,128)(4,1)S(1)} %fusion.151), kind=kOutput, calls=%fused_computation.24.clone.1 | convolution fusion | flops 555661440 | bytes 35912704 | tf_op jit(solution)/shard_map/while/body/eval_jaxpr/qhd,khd->hqk/dot_general | solution.py:146
  579.7 11.4 %multiply_convert_fusion.4 = bf16[3,640,2176]{2,1,0:T(8,128)(2,1)S(1)} fusion(f32[3,640,2176]{2,1,0:T(8,128)} %get-tuple-element.583, f32[3,640,2176]{2,1,0:T(8,128)} %fusion.150, f32[3,640]{1,0:T(4,128)S(1)} %get-tuple-element.584), kind=kLoop, calls=%fused_computation.23.clone.1 | loop fusion | flops 12533760 | bytes 41786880 | tf_op jit(solution)/shard_map/while/body/eval_jaxpr/convert_element_type | solution.py:228
  591.1 3.9 copy-done
  600.7 4.4 fusion.153
  611.3 26.8 %collective-permute-done.3 = bf16[256,384]{0,1:T(8,128)(2,1)S(1)} collective-permute-done((bf16[256,384]{0,1:T(8,128)(2,1)S(1)}, bf16[256,384]{0,1:T(8,128)(2,1)S(1)}, u32[]{:S(2)}, u32[]{:S(2)}) %collective-permute-start.3) | collective-permute-done | bytes 196640 | tf_op jit(solution)/shard_map/ppermute | solution.py:16
  643.2 4.0 multiply_convert_fusion.1
  650.1 4.3 all-to-all-start.4
  654.4 4.3 convolution_convert_fusion.2
  671.4 10.9 %all-to-all-done.4 = bf16[8,768,96]{1,2,0:T(8,128)(2,1)} async-done(((bf16[8,768,96]{1,2,0:T(8,128)(2,1)}), bf16[8,768,96]{1,2,0:T(8,128)(2,1)}, u32[]{:S(2)}, u32[]{:S(2)}) %all-to-all-start.4) | async-done | bytes 1179680 | tf_op jit(solution)/shard_map/all_to_all | solution.py:27
  682.3 4.1 all-to-all-start.2
  690.4 6.3 all-reduce.4
  699.8 6.2 all-to-all-start.1
  705.9 4.9 convolution_convert_fusion.8
  714.3 15.6 %all-to-all-done.1 = bf16[8,96,577]{2,1,0:T(8,128)(2,1)S(1)} async-done(((bf16[8,96,577]{2,1,0:T(8,128)(2,1)}), bf16[8,96,577]{2,1,0:T(8,128)(2,1)S(1)}, u32[]{:S(2)}, u32[]{:S(2)}) %all-to-all-start.1) | async-done | bytes 886304 | tf_op jit(solution)/shard_map/all_to_all | solution.py:27
  742.9 24.3 %all-to-all-done.3 = bf16[8,96,769]{2,1,0:T(8,128)(2,1)S(1)} async-done(((bf16[8,96,769]{2,1,0:T(8,128)(2,1)}), bf16[8,96,769]{2,1,0:T(8,128)(2,1)S(1)}, u32[]{:S(2)}, u32[]{:S(2)}) %all-to-all-start.3) | async-done | bytes 1181216 | tf_op jit(solution)/shard_map/all_to_all | solution.py:27
  (244 shorter events, 121.7 us)
Async XLA Ops:
  8.0 95.4 %all-gather.6.cloned.1.call-start = ((), (), s32[]{:S(2)}) async-start(), calls=%async_computation.9 | async-start | bytes 2457600 | tf_op jit(solution)/shard_map/all_gather | solution.py:101
  9.3 30.9 %copy-start.37 = (f32[320]{0:T(512)}, f32[320]{0:T(512)S(1)}, u32[]{:S(2)}) copy-start(f32[320]{0:T(512)S(1)} %add_rsqrt_fusion.1) | copy-start | bytes 3844
  39.2 264.5 %reduce-scatter.5.cloned.1.call-start = ((), (), s32[]{:S(2)}) async-start(), calls=%async_computation.10 | async-start | bytes 2457600 | tf_op jit(solution)/shard_map/reduce_scatter | solution.py:165
  72.2 36.3 %copy-start.20 = (bf16[768,192]{1,0:T(8,128)(2,1)}, bf16[768,192]{1,0:T(8,128)(2,1)S(1)}, u32[]{:S(2)}) copy-start(bf16[768,192]{1,0:T(8,128)(2,1)S(1)} %all_gather.35) | copy-start | bytes 884740
  103.4 52.9 %copy-start.22 = (bf16[768,192]{1,0:T(8,128)(2,1)}, bf16[768,192]{1,0:T(8,128)(2,1)S(1)}, u32[]{:S(2)}) copy-start(bf16[768,192]{1,0:T(8,128)(2,1)S(1)} %all_gather.36) | copy-start | bytes 884740
  103.4 6.5 copy-start.29
  103.4 6.6 copy-start.43
  103.4 52.9 %copy-start.36 = (bf16[96,192]{1,0:T(8,128)(2,1)S(1)}, bf16[96,192]{1,0:T(8,128)(2,1)}, u32[]{:S(2)}) copy-start(bf16[96,192]{1,0:T(8,128)(2,1)} %param.21) | copy-start | bytes 110596
  105.9 82.6 %copy-start.3 = (bf16[1280,768]{1,0:T(8,128)(2,1)S(1)}, bf16[1280,768]{1,0:T(8,128)(2,1)}, u32[]{:S(2)}) copy-start(bf16[1280,768]{1,0:T(8,128)(2,1)} %all-gather.6.cloned.1.call-done) | copy-start | bytes 5898244
  108.5 83.2 %collective-permute-start.1 = (bf16[1280,384]{0,1:T(8,128)(2,1)S(1)}, bf16[1280,384]{0,1:T(8,128)(2,1)S(1)}, u32[]{:S(2)}, u32[]{:S(2)}) collective-permute-start(bf16[1280,384]{0,1:T(8,128)(2,1)S(1)} %pad_maximum_fusion.1), channel_id=1, source_target_pairs={{0,4},{4,8},{8,12},{12,16},{16,20},{20,24},{24,28},{1,5},{5,9},{9,... | collective-permute-start | bytes 2949128 | tf_op jit(solution)/shard_map/ppermute | solution.py:16
  187.2 4.5 collective-permute-start
  219.8 8.9 %copy-start.27 = (bf16[2,640,192]{1,2,0:T(8,128)(2,1)S(1)}, bf16[2,640,192]{1,2,0:T(8,128)(2,1)}, u32[]{:S(2)}) copy-start(bf16[2,640,192]{1,2,0:T(8,128)(2,1)} %get-tuple-element.602) | copy-start | bytes 1474564 | tf_op jit(solution)/shard_map/while
  256.0 8.9 %copy-start.27 = (bf16[2,640,192]{1,2,0:T(8,128)(2,1)S(1)}, bf16[2,640,192]{1,2,0:T(8,128)(2,1)}, u32[]{:S(2)}) copy-start(bf16[2,640,192]{1,2,0:T(8,128)(2,1)} %get-tuple-element.602) | copy-start | bytes 1474564 | tf_op jit(solution)/shard_map/while
  265.7 38.0 %copy-start.1 = (bf16[320,768]{1,0:T(8,128)(2,1)S(1)}, bf16[320,768]{1,0:T(8,128)(2,1)}, u32[]{:S(2)}) copy-start(bf16[320,768]{1,0:T(8,128)(2,1)} %param.16) | copy-start | bytes 1474564
  266.9 40.2 %copy-start.11 = (bf16[2,24,8,640]{3,2,0,1:T(8,128)(2,1)}, bf16[2,24,8,640]{3,2,0,1:T(8,128)(2,1)S(1)}, u32[]{:S(2)}) copy-start(bf16[2,24,8,640]{3,2,0,1:T(8,128)(2,1)S(1)} %copy.67) | copy-start | bytes 1474564
  270.1 47.0 %all-gather.10.cloned.1.call-start = ((), (), s32[]{:S(2)}) async-start(), calls=%async_computation.12 | async-start | bytes 1327104 | tf_op jit(solution)/shard_map/all_gather | solution.py:82
  270.7 68.7 %all-gather.8.cloned.1.call-start = ((), (), s32[]{:S(2)}) async-start(), calls=%async_computation.11 | async-start | bytes 2457600 | tf_op jit(solution)/shard_map/all_gather | solution.py:174
  271.0 186.0 %copy-start.30 = (f32[768]{0:T(1024)}, f32[768]{0:T(1024)S(1)}, u32[]{:S(2)}) copy-start(f32[768]{0:T(1024)S(1)} %convert_element_type.159) | copy-start | bytes 9220
  305.0 152.0 %copy-start.34 = (f32[320]{0:T(512)}, f32[320]{0:T(512)S(1)}, u32[]{:S(2)}) copy-start(f32[320]{0:T(512)S(1)} %add_rsqrt_fusion) | copy-start | bytes 3844
  307.1 76.2 %all-gather.12.cloned.1.call-start = ((), (), s32[]{:S(2)}) async-start(), calls=%async_computation.13 | async-start | bytes 1327104 | tf_op jit(solution)/shard_map/all_gather | solution.py:83
  307.6 97.5 %all-gather.14.cloned.1.call-start = ((), (), s32[]{:S(2)}) async-start(), calls=%async_computation.15 | async-start | bytes 2457600 | tf_op jit(solution)/shard_map/all_gather | solution.py:184
  308.4 146.4 %reduce-scatter.9.cloned.1.call-start = ((), (), s32[]{:S(2)}) async-start(), calls=%async_computation.16 | async-start | bytes 2457600 | tf_op jit(solution)/shard_map/reduce_scatter | solution.py:194
  419.6 35.2 %copy-start.6 = (bf16[320,768]{1,0:T(8,128)(2,1)S(1)}, bf16[320,768]{1,0:T(8,128)(2,1)}, u32[]{:S(2)}) copy-start(bf16[320,768]{1,0:T(8,128)(2,1)} %reduce-scatter.5.cloned.1.call-done) | copy-start | bytes 1474564
  419.6 37.4 %copy-start.8 = (bf16[320,768]{1,0:T(8,128)(2,1)S(1)}, bf16[320,768]{1,0:T(8,128)(2,1)}, u32[]{:S(2)}) copy-start(bf16[320,768]{1,0:T(8,128)(2,1)} %param.17) | copy-start | bytes 1474564
  457.0 30.8 %copy-start.26 = (bf16[192,768]{0,1:T(8,128)(2,1)S(1)}, bf16[192,768]{0,1:T(8,128)(2,1)}, u32[]{:S(2)}) copy-start(bf16[192,768]{0,1:T(8,128)(2,1)} %all_gather.38) | copy-start | bytes 884740
  459.9 27.9 %all-to-all-start = ((bf16[4,320,768]{2,1,0:T(8,128)(2,1)}), bf16[4,320,768]{2,1,0:T(8,128)(2,1)S(1)}, u32[]{:S(2)}, u32[]{:S(2)}) async-start(bf16[4,320,768]{2,1,0:T(8,128)(2,1)} %stack.2), calls=%async_computation.3 | async-start | bytes 3932160 | tf_op jit(solution)/shard_map/all_to_all | solution.py:205
  463.5 225.3 %reduce-scatter.11.cloned.1.call-start = ((), (), s32[]{:S(2)}) async-start(), calls=%async_computation.17 | async-start | bytes 2457600 | tf_op jit(solution)/shard_map/reduce_scatter | solution.py:283
  523.4 15.3 %copy-start = (f32[3,640,2176]{2,1,0:T(8,128)S(1)}, f32[3,640,2176]{2,1,0:T(8,128)}, u32[]{:S(2)}) copy-start(f32[3,640,2176]{2,1,0:T(8,128)} %get-tuple-element.583) | copy-start | bytes 50135044 | tf_op jit(solution)/shard_map/while
  579.7 15.3 %copy-start = (f32[3,640,2176]{2,1,0:T(8,128)S(1)}, f32[3,640,2176]{2,1,0:T(8,128)}, u32[]{:S(2)}) copy-start(f32[3,640,2176]{2,1,0:T(8,128)} %get-tuple-element.583) | copy-start | bytes 50135044 | tf_op jit(solution)/shard_map/while
  607.7 30.3 %collective-permute-start.2 = (bf16[1280,384]{0,1:T(8,128)(2,1)S(1)}, bf16[1280,384]{0,1:T(8,128)(2,1)S(1)}, u32[]{:S(2)}, u32[]{:S(2)}) collective-permute-start(bf16[1280,384]{0,1:T(8,128)(2,1)S(1)} %slice.58), channel_id=1, source_target_pairs={{4,0},{8,4},{12,8},{16,12},{20,16},{24,20},{28,24},{5,1},{9,5},{13... | collective-permute-start | bytes 2949128 | tf_op jit(solution)/shard_map/ppermute | solution.py:16
  609.2 28.8 %collective-permute-start.3 = (bf16[256,384]{0,1:T(8,128)(2,1)S(1)}, bf16[256,384]{0,1:T(8,128)(2,1)S(1)}, u32[]{:S(2)}, u32[]{:S(2)}) collective-permute-start(bf16[256,384]{0,1:T(8,128)(2,1)S(1)} %slice.59), channel_id=1, source_target_pairs={{8,0},{12,4},{16,8},{20,12},{24,16},{28,20},{9,1},{13,5},{17,9},{2... | collective-permute-start | bytes 589832 | tf_op jit(solution)/shard_map/ppermute | solution.py:16
  610.5 29.3 %copy-start.21 = (bf16[768,192]{1,0:T(8,128)(2,1)S(1)}, bf16[768,192]{1,0:T(8,128)(2,1)}, u32[]{:S(2)}) copy-start(bf16[768,192]{1,0:T(8,128)(2,1)} %copy-done.20) | copy-start | bytes 884740
  650.1 32.2 %all-to-all-start.4 = ((bf16[8,768,96]{1,2,0:T(8,128)(2,1)}), bf16[8,768,96]{1,2,0:T(8,128)(2,1)}, u32[]{:S(2)}, u32[]{:S(2)}) async-start(bf16[8,768,96]{1,2,0:T(8,128)(2,1)} %bitcast.157), calls=%async_computation.8 | async-start | bytes 2359296 | tf_op jit(solution)/shard_map/all_to_all | solution.py:27
  654.3 84.0 %reduce-scatter.7.cloned.1.call-start = ((), (), s32[]{:S(2)}) async-start(), calls=%async_computation.14 | async-start | bytes 2457600 | tf_op jit(solution)/shard_map/reduce_scatter | solution.py:177
  662.9 23.4 %copy-start.19 = (bf16[1280,384]{0,1:T(8,128)(2,1)S(1)}, bf16[1280,384]{0,1:T(8,128)(2,1)}, u32[]{:S(2)}) copy-start(bf16[1280,384]{0,1:T(8,128)(2,1)} %copy-done.18) | copy-start | bytes 2949124
  667.1 21.7 %copy-start.2 = (bf16[320,768]{1,0:T(8,128)(2,1)S(1)}, bf16[320,768]{1,0:T(8,128)(2,1)}, u32[]{:S(2)}) copy-start(bf16[320,768]{1,0:T(8,128)(2,1)} %param.16) | copy-start | bytes 1474564
  667.1 21.7 %copy-start.33 = (f32[768]{0:T(1024)S(1)}, f32[768]{0:T(1024)}, u32[]{:S(2)}) copy-start(f32[768]{0:T(1024)} %copy-done.32) | copy-start | bytes 9220
  667.1 21.7 %copy-start.38 = (f32[320]{0:T(512)S(1)}, f32[320]{0:T(512)}, u32[]{:S(2)}) copy-start(f32[320]{0:T(512)} %copy-done.37) | copy-start | bytes 3844
  667.1 23.3 %copy-start.41 = (f32[768]{0:T(1024)S(1)}, f32[768]{0:T(1024)}, u32[]{:S(2)}) copy-start(f32[768]{0:T(1024)} %get-tuple-element.370) | copy-start | bytes 9220
  682.3 17.5 %all-to-all-start.2 = ((bf16[8,192,96]{2,1,0:T(8,128)(2,1)}), bf16[8,192,96]{2,1,0:T(8,128)(2,1)}, u32[]{:S(2)}, u32[]{:S(2)}) async-start(bf16[8,192,96]{2,1,0:T(8,128)(2,1)} %bitcast.153), calls=%async_computation.6 | async-start | bytes 786432 | tf_op jit(solution)/shard_map/all_to_all | solution.py:27
  699.8 30.1 %all-to-all-start.1 = ((bf16[8,96,577]{2,1,0:T(8,128)(2,1)}), bf16[8,96,577]{2,1,0:T(8,128)(2,1)S(1)}, u32[]{:S(2)}, u32[]{:S(2)}) async-start(bf16[8,96,577]{2,1,0:T(8,128)(2,1)} %pad_maximum_fusion.2), calls=%async_computation.5 | async-start | bytes 1966080 | tf_op jit(solution)/shard_map/all_to_all | solution.py:27
  710.8 27.5 %copy-start.7 = (bf16[320,768]{1,0:T(8,128)(2,1)S(1)}, bf16[320,768]{1,0:T(8,128)(2,1)}, u32[]{:S(2)}) copy-start(bf16[320,768]{1,0:T(8,128)(2,1)} %reduce-scatter.5.cloned.1.call-done) | copy-start | bytes 1474564
  710.8 27.5 %copy-start.9 = (bf16[320,768]{1,0:T(8,128)(2,1)S(1)}, bf16[320,768]{1,0:T(8,128)(2,1)}, u32[]{:S(2)}) copy-start(bf16[320,768]{1,0:T(8,128)(2,1)} %param.17) | copy-start | bytes 1474564
  710.8 27.5 %copy-start.10 = (bf16[320,768]{1,0:T(8,128)(2,1)S(1)}, bf16[320,768]{1,0:T(8,128)(2,1)}, u32[]{:S(2)}) copy-start(bf16[320,768]{1,0:T(8,128)(2,1)} %reduce-scatter.9.cloned.1.call-done) | copy-start | bytes 1474564
  710.8 27.5 %copy-start.31 = (f32[768]{0:T(1024)S(1)}, f32[768]{0:T(1024)}, u32[]{:S(2)}) copy-start(f32[768]{0:T(1024)} %copy-done.30) | copy-start | bytes 9220
  710.9 27.5 %copy-start.35 = (f32[320]{0:T(512)S(1)}, f32[320]{0:T(512)}, u32[]{:S(2)}) copy-start(f32[320]{0:T(512)} %copy-done.34) | copy-start | bytes 3844
  710.9 27.5 %copy-start.40 = (f32[320]{0:T(512)S(1)}, f32[320]{0:T(512)}, u32[]{:S(2)}) copy-start(f32[320]{0:T(512)} %copy-done.39) | copy-start | bytes 3844
  730.8 36.4 %all-to-all-start.3 = ((bf16[8,96,769]{2,1,0:T(8,128)(2,1)}), bf16[8,96,769]{2,1,0:T(8,128)(2,1)S(1)}, u32[]{:S(2)}, u32[]{:S(2)}) async-start(bf16[8,96,769]{2,1,0:T(8,128)(2,1)} %pad_maximum_fusion), calls=%async_computation.7 | async-start | bytes 2752512 | tf_op jit(solution)/shard_map/all_to_all | solution.py:27
  (21 other events, 62.5 us)
Sparse Core Ops, SparseCore 0:
  39.3 19.0 all-gather.5
  270.2 33.4 reduce-scatter.4
  424.1 30.6 reduce-scatter.8
Sparse Core Ops, SparseCore 1:
  272.8 44.3 all-gather.9
  319.2 20.1 all-gather.7
  341.7 41.5 all-gather.11
  384.9 20.1 all-gather.13
  643.3 28.8 reduce-scatter.10
  674.9 30.8 reduce-scatter.6
